TPU v7x, 512 devices: a whole 4x4x16 slice. The times are simulated.
512 devices in a mesh: row: 32 (over z_hi, y, core), col: 16 (over z_lo, x).
Axes of the slice: x: 4, y: 4, z: 16 (z_hi: 4, z_lo: 4; z = z_hi * 4 + z_lo), core: 2. Of those that a mesh axis runs over, the one named last changes fastest.
Arguments:
- star_phase: float32 [9, 65536], P(None, ('row', 'col')), may hold values from -6 to 6
- star_mass: float32 [65536], P(('row', 'col')), may hold values from 0.25 to 4
- due_mask: int32 [65536], P(('row', 'col')), may hold values 0 or 1
Outputs:
- derivatives: float32 [9, 65536], P(None, ('row', 'col'))
Inputs may be any that keep to these rules, and one draw needn't show every extreme that they name: `due_mask`: 1 marks a due star.
All inputs are finite; a program needn't handle non-finite values. No bound on the sum of `due_mask` on one device may be relied on, other than what follows from the above.
Results may differ from a plain program's by a relative error of at most 0.00016.
Values sent between devices are 32-bit elements; how exact they have to be, the bound alone decides.
No kernel may reach another device: no remote copies, remote signals or barrier semaphores. Data moves between devices by JAX's collectives and lax.ppermute only.
A program may use at most 64 MiB of HBM per device.

v0:
```python
import jax
import jax.numpy as jnp
from jax import lax
from jax.sharding import PartitionSpec as P

softening = 0.01


def from_root(value, axis, root):
    mine = lax.axis_index(axis) == root
    return lax.psum(jnp.where(mine, value, jnp.zeros_like(value)), axis)


def pair_field(targets, sources):
    deltas = [sources[component][None, :] - targets[component][:, None] for component in range(9)]
    spread = deltas[0] * deltas[0] + deltas[1] * deltas[1] + deltas[2] * deltas[2] + softening
    reciprocal = lax.rsqrt(spread)
    recip_square = reciprocal * reciprocal
    recip_cube = reciprocal * recip_square
    radial_rate = (
        deltas[0] * deltas[3] + deltas[1] * deltas[4] + deltas[2] * deltas[5]
    ) * recip_square
    second_rate = (
        deltas[3] * deltas[3]
        + deltas[4] * deltas[4]
        + deltas[5] * deltas[5]
        + deltas[0] * deltas[6]
        + deltas[1] * deltas[7]
        + deltas[2] * deltas[8]
    ) * recip_square
    second_rate = second_rate + radial_rate * radial_rate
    accel = [deltas[component] * recip_cube for component in range(3)]
    jerk_part = [
        deltas[component + 3] * recip_cube - 3.0 * radial_rate * accel[component]
        for component in range(3)
    ]
    snap_part = [
        deltas[component + 6] * recip_cube
        - 6.0 * radial_rate * jerk_part[component]
        - 3.0 * second_rate * accel[component]
        for component in range(3)
    ]
    return accel + jerk_part + snap_part


def pair_sums(first_phase, first_mass, second_phase, second_mass):
    first_count = first_phase.shape[1]
    second_count = second_phase.shape[1]
    height = min(128, first_count)
    turns = first_count // height
    first_blocks = first_phase.reshape(9, turns, height).transpose(1, 0, 2)
    mass_blocks = first_mass.reshape(turns, height)

    def one_turn(carry, item):
        block_rows, block_mass = item
        fields = pair_field(block_rows, second_phase)
        onward = jnp.stack(
            [jnp.sum(field_term * second_mass[None, :], axis=1) for field_term in fields]
        )
        backward = jnp.stack(
            [jnp.sum(field_term * block_mass[:, None], axis=0) for field_term in fields]
        )
        return (carry - backward, onward)

    start = jnp.zeros((9, second_count), jnp.float32)
    reaction, onwards = lax.scan(one_turn, start, (first_blocks, mass_blocks))
    return (onwards.transpose(1, 0, 2).reshape(9, first_count), reaction)


def rows_finish(moved):
    items = moved.shape[4]
    flat = moved.reshape(9, moved.shape[1] * moved.shape[2], items)
    returned = lax.all_to_all(flat, "row", split_axis=1, concat_axis=1, tiled=True)
    return jnp.sum(returned, axis=1)


def on_device(star_phase, star_mass, due_mask):
    row_count = lax.axis_size("row")
    col_count = lax.axis_size("col")
    row_index = lax.axis_index("row")
    col_index = lax.axis_index("col")
    targets, target_mass = (
        lax.all_gather(star_phase, "col", axis=1, tiled=True),
        lax.all_gather(star_mass, "col", axis=1 - 1, tiled=True),
    )
    block = targets.shape[1]
    half = block // 2
    piece = block // col_count
    low_phase, high_phase = (targets[:, :half], targets[:, half:])
    low_mass, high_mass = (target_mass[:half], target_mass[half:])
    empty_block = jnp.zeros((9, block), jnp.float32)
    own_total = jnp.zeros((9, block), jnp.float32)
    reactions = []
    for which in range(2):
        source_phase, source_mass = (
            from_root(targets, "row", 2 * col_index + which),
            from_root(target_mass, "row", 2 * col_index + which),
        )
        source_index = 2 * col_index + which
        case = jnp.where(
            row_index < source_index, 2, jnp.where(row_index == source_index, 1, 0)
        ).astype(jnp.int32)

        def diagonal_cell(source_phase=source_phase, source_mass=source_mass):
            own_low, unused_low = pair_sums(low_phase, low_mass, source_phase, source_mass)
            own_high, unused_high = pair_sums(high_phase, high_mass, source_phase, source_mass)
            return (jnp.concatenate([own_low, own_high], axis=1), empty_block)

        def upper_cell(source_phase=source_phase, source_mass=source_mass):
            own_low, back_low = pair_sums(low_phase, low_mass, source_phase, source_mass)
            own_high, back_high = pair_sums(high_phase, high_mass, source_phase, source_mass)
            return (jnp.concatenate([own_low, own_high], axis=1), back_low + back_high)

        def lower_cell(source_phase=source_phase, source_mass=source_mass):
            return (empty_block, empty_block)

        own_cell, reaction_cell = lax.switch(case, [lower_cell, diagonal_cell, upper_cell])
        own_total = own_total + own_cell
        reactions.append(reaction_cell)
    reaction_all = jnp.concatenate(reactions, axis=1).reshape(9, 1, 2, col_count, piece)
    own_piece = lax.psum_scatter(own_total, "col", scatter_dimension=1, tiled=True)
    reaction_piece = rows_finish(
        lax.all_to_all(reaction_all, "col", split_axis=3, concat_axis=1, tiled=True)
    )
    totals = own_piece + reaction_piece
    stars_total = jnp.float32(block * row_count)
    return totals / stars_total * due_mask.astype(jnp.float32)[None, :]


def solution(mesh):
    in_specs = (P(None, ("row", "col")), P(("row", "col")), P(("row", "col")))
    out_specs = P(None, ("row", "col"))
    return jax.shard_map(
        on_device, mesh=mesh, in_specs=in_specs, out_specs=out_specs, check_vma=False
    )
```

profile of v0, /device:TPU:24, one launch (start us, length us, event | category | flops | bytes accessed | tf_op | source)
XLA Modules:
  0.0 786.7 jit_solution(2250065482413114201)
XLA Ops:
  6.5 0.0 all-reduce.4.cloned.1.call-start
  6.5 0.0 copy-start.3
  6.5 0.7 copy-done.3
  7.2 44.2 %all_gather.6 = f32[9,2048]{1,0:T(8,128)S(1)} all-gather(f32[9,128]{1,0:T(8,128)S(1)} %copy-done.3), channel_id=1, replica_groups=mesh['row'=32,'col'=16] {'col'}, dimensions={1}, use_global_device_ids=true | all-gather | bytes 78336 | tf_op jit(solution)/shard_map/all_gather | solution.py:83
  51.4 0.7 broadcast_select_fusion
  52.1 0.0 all-reduce.4.cloned.1.call-update
  52.2 0.0 copy-start.4
  52.2 0.6 copy-done.4
  52.9 36.5 %all-gather = f32[16,1,128]{2,1,0:T(1,128)S(1)} all-gather(f32[1,1,128]{2,1,0:T(1,128)S(1)} %bitcast.1253), channel_id=1, replica_groups=mesh['row'=32,'col'=16] {'col'}, dimensions={0}, use_global_device_ids=true | all-gather | bytes 8704 | tf_op jit(solution)/shard_map/all_gather | solution.py:84
  89.4 159.6 %all-reduce = (f32[2048]{0:T(1024)S(1)}, f32[2048]{0:T(1024)S(1)}) all-reduce(f32[2048]{0:T(1024)S(1)} %bitcast.1172, f32[2048]{0:T(1024)S(1)} %bitcast.1171), channel_id=1, replica_groups=mesh['row'=32,'col'=16] {'row'}, use_global_device_ids=true, to_apply=%region_1.2 | all-reduce | flops 4096 | bytes 32768 | tf_op jit(solution)/shard_map/psum | solution.py:11
  249.0 145.8 %all-reduce.4.cloned.1.call-done = (f32[9,2048]{1,0:T(8,128)}, f32[9,2048]{1,0:T(8,128)}) async-done(((f32[9,2048]{1,0:T(8,128)}, f32[9,2048]{1,0:T(8,128)}), (f32[9,2048]{1,0:T(8,128)}, f32[9,2048]{1,0:T(8,128)})) %all-reduce.4.cloned.1.call-update) | async-done | bytes 147472 | tf_op jit(solution)/shard_map/psum | solution.py:11
  394.7 0.0 copy-start
  394.7 0.9 copy-done
  395.6 0.3 conditional.3
  395.9 0.4 conditional.2
  396.3 0.1 copy.181
  396.4 0.1 copy.82
  396.5 277.2 %all_to_all.20 = f32[9,1,2,16,128]{4,2,0,1,3:T(2,128)S(1)} all-to-all(f32[9,1,2,16,128]{4,2,0,1,3:T(2,128)S(1)} %copy.82), channel_id=1, replica_groups=mesh['row'=32,'col'=16] {'col'}, dimensions={3} | all-to-all | bytes 294912 | tf_op jit(solution)/shard_map/all_to_all | solution.py:123
  673.6 0.1 copy.83
  673.7 0.8 copy.84
  674.5 13.1 %all-to-all-start.1 = ((f32[9,32,128]{2,0,1:T(8,128)}), f32[9,32,128]{2,0,1:T(8,128)S(1)}, u32[]{:S(2)}, u32[]{:S(2)}) async-start(f32[9,32,128]{2,0,1:T(8,128)} %copy.84), calls=%async_computation.2 | async-start | bytes 524288 | tf_op jit(solution)/shard_map/all_to_all | solution.py:73
  687.6 0.0 reduce-scatter.2.cloned.1.call-start
  687.7 0.7 add.316
  688.3 0.0 copy-start.5
  688.3 0.0 reduce-scatter.2.cloned.1.call-update
  688.4 0.6 copy-done.5
  689.0 17.3 %all-to-all-done.1 = f32[9,32,128]{2,0,1:T(8,128)S(1)} async-done(((f32[9,32,128]{2,0,1:T(8,128)}), f32[9,32,128]{2,0,1:T(8,128)S(1)}, u32[]{:S(2)}, u32[]{:S(2)}) %all-to-all-start.1) | async-done | bytes 147488 | tf_op jit(solution)/shard_map/all_to_all | solution.py:73
  706.3 72.2 %reduce-scatter.2.cloned.1.call-done = f32[9,128]{1,0:T(8,128)} async-done(((f32[9,2048]{1,0:T(8,128)}), f32[9,128]{1,0:T(8,128)}) %reduce-scatter.2.cloned.1.call-update) | async-done | bytes 4624 | tf_op jit(solution)/shard_map/reduce_scatter | solution.py:121
  778.5 1.3 add_multiply_fusion
  (11 shorter events, 0.1 us)
Async XLA Ops:
  6.5 388.2 %all-reduce.4.cloned.1.call-start = ((), (), s32[]{:S(2)}) async-start(), calls=%async_computation.4 | async-start | bytes 524288 | tf_op jit(solution)/shard_map/psum | solution.py:11
  6.5 0.7 copy-start.3
  52.2 0.7 copy-start.4
  394.7 0.9 copy-start
  674.5 31.8 %all-to-all-start.1 = ((f32[9,32,128]{2,0,1:T(8,128)}), f32[9,32,128]{2,0,1:T(8,128)S(1)}, u32[]{:S(2)}, u32[]{:S(2)}) async-start(f32[9,32,128]{2,0,1:T(8,128)} %copy.84), calls=%async_computation.2 | async-start | bytes 524288 | tf_op jit(solution)/shard_map/all_to_all | solution.py:73
  687.6 90.9 %reduce-scatter.2.cloned.1.call-start = ((), (), s32[]{:S(2)}) async-start(), calls=%async_computation.3 | async-start | bytes 139264 | tf_op jit(solution)/shard_map/reduce_scatter | solution.py:121
  688.3 0.7 copy-start.5
Sparse Core Ops, SparseCore 0:
  52.3 342.4 all-reduce.3
  691.5 87.0 reduce-scatter.1
where the time goes:
time: 794 us; the launch traced here: 787 us
  blocking collectives  517 us (65%)
  waiting for transfers between devices  235 us (30%)
  between operations  13.5 us (2%)
  starting transfers between devices  13.2 us (2%)
    all_to_all x1, blocking collectives, on_device(): lax.all_to_all(reaction_all, 'col', split_axis=3, concat_axis=1, tiled=True)  277 us
    psum x1, blocking collectives, from_root(): return lax.psum(jnp.where(mine, value, jnp.zeros_like(value)), axis)  160 us
    psum x1, waiting for transfers between devices, from_root(): return lax.psum(jnp.where(mine, value, jnp.zeros_like(value)), axis)  146 us
    reduce_scatter x1, waiting for transfers between devices, on_device(): lax.psum_scatter(own_total, 'col', scatter_dimension=1, tiled=True)  72.2 us
    all_gather x1, blocking collectives, on_device(): lax.all_gather(star_phase, 'col', axis=1, tiled=True)  44.2 us
    all_gather x1, blocking collectives, on_device(): lax.all_gather(star_mass, 'col', axis=1 - 1, tiled=True)  36.5 us
    all_to_all x1, waiting for transfers between devices, rows_finish(): lax.all_to_all(flat, 'row', split_axis=1, concat_axis=1, tiled=True)  17.3 us
  transfers between devices with their start and end apart: 3, of which 3 were waited for; matrix products, arithmetic and copies ran while one was open for 0% of the time, Pallas kernels for 0%

commit v1 on v0

v1 whole, which is shorter than its diff:
```python
import functools

import jax
import jax.numpy as jnp
from jax import lax
from jax.experimental import pallas as pl
from jax.experimental.pallas import tpu as pltpu
from jax.sharding import PartitionSpec as P

F32 = jnp.float32
BF16 = jnp.bfloat16
SOFTENING = 0.01
LANES = 128
WIDE = 4
COMBOS = ("hh", "hm", "mh", "mm", "hl", "lh")


def split3(value):
    high = value.astype(BF16)
    rest = value - high.astype(F32)
    middle = rest.astype(BF16)
    low = (rest - middle.astype(F32)).astype(BF16)
    return {"h": high, "m": middle, "l": low}


def dot(left, right):
    return jnp.dot(left, right, preferred_element_type=F32)


def pair_kernel(
    tile_i, tile_j, targets, sources, out, stage, left_rate, left_second,
    right_rate, right_second, feat_c, feat_p, feat_u, place, totals
):
    target_blocks, source_blocks = targets.shape[0], sources.shape[0]
    target_count, source_count = target_blocks * LANES, source_blocks * LANES
    width = WIDE * LANES

    def rows(ref, block, low, high):
        return jnp.concatenate([ref[block * WIDE + k, low:high, :] for k in range(WIDE)], axis=1)

    def put(pieces, height):
        stage[0:height, :] = jnp.zeros((height, width), F32)
        for at, piece in pieces:
            stage[at : at + piece.shape[0], :] = piece
        return split3(stage[0:height, :])

    one = jnp.ones((1, width), F32)

    def prepare_sources(block, carry):
        lanes = pl.ds(pl.multiple_of(block * width, width), width)
        x, v, a = (rows(sources, block, k, k + 3) for k in (0, 3, 6))
        m = rows(sources, block, 9, 10)
        x_v = jnp.sum(x * v, axis=0, keepdims=True)
        second = jnp.sum(v * v + x * a, axis=0, keepdims=True)
        parts = put([(0, v), (3, x), (6, one), (7, x_v)], 16)
        right_rate[:, lanes] = jnp.concatenate([parts[c[1]] for c in COMBOS], axis=0)
        parts = put([(0, 0.2 * v), (3, 0.2 * a), (6, 0.2 * x), (9, one), (10, 0.2 * second)], 16)
        right_second[:, lanes] = jnp.concatenate([parts[c[1]] for c in COMBOS], axis=0)
        empty = jnp.zeros((32, width), F32)
        mx, mv = m * x, m * v
        for ref, pieces in (
            (feat_c, [(0, m), (1, mx), (4, mv), (7, m * a)]),
            (feat_p, [(10, m), (11, mx), (14, mv)]),
            (feat_u, [(17, m), (18, mx)]),
        ):
            parts = put(pieces, 32)
            tall = jnp.concatenate([parts[k].astype(F32) for k in "hml"] + [empty], axis=0)
            ref[lanes, :] = tall.T.astype(BF16)
        return carry

    def prepare_targets(block, carry):
        lanes = pl.ds(pl.multiple_of(block * width, width), width)
        x, v, a = (rows(targets, block, k, k + 3) for k in (0, 3, 6))
        x_v = jnp.sum(x * v, axis=0, keepdims=True)
        second = jnp.sum(v * v + x * a, axis=0, keepdims=True)
        empty = jnp.zeros((32, width), F32)
        for ref, pieces in (
            (left_rate, [(0, -x), (3, -v), (6, x_v), (7, one)]),
            (left_second, [(0, -2.0 * v), (3, -x), (6, -a), (9, 0.2 * second), (10, one)]),
        ):
            parts = put(pieces, 16)
            tall = jnp.concatenate([parts[c[0]].astype(F32) for c in COMBOS] + [empty], axis=0)
            ref[lanes, :] = tall.T.astype(BF16)
        for k in range(3):
            place[k, lanes, :] = jnp.broadcast_to(x[k : k + 1, :], (LANES, width)).T
        return carry

    lax.fori_loop(0, source_blocks // WIDE, prepare_sources, 0)
    lax.fori_loop(0, target_blocks // WIDE, prepare_targets, 0)
    totals[...] = jnp.zeros_like(totals)

    def column(block, carry):
        js = pl.ds(pl.multiple_of(block * tile_j, tile_j), tile_j)
        xs=[jnp.concatenate([sources[block*(tile_j//LANES)+q,k:k+1,:] for q in range(tile_j//LANES)],axis=1) for k in range(3)]
        for turn in range(target_count // tile_i):
            is_ = pl.ds(turn * tile_i, tile_i)
            rate = dot(left_rate[is_, 0:96], right_rate[:, js])
            second = dot(left_second[is_, 0:96], right_second[:, js])
            spread = None
            for k in range(3):
                here = jnp.concatenate([place[k, is_, :]] * (tile_j // LANES), axis=1)
                delta = xs[k] - here
                spread = delta * delta + SOFTENING if spread is None else spread + delta * delta
            recip = lax.rsqrt(spread)
            square = recip * recip
            cube = recip * square
            p = rate * square
            added = None
            for weight, feat in (
                (cube, feat_c), (p * cube, feat_p), ((p * p - second * square) * cube, feat_u)
            ):
                high = weight.astype(BF16)
                low = (weight - high.astype(F32)).astype(BF16)
                part = dot(high, feat[js, :]) + dot(low, feat[js, :])
                added = part if added is None else added + part
            totals[is_, :] += added
        return carry

    lax.fori_loop(0, source_count // tile_j, column, 0)

    def finish(block, carry):
        t = totals[pl.ds(pl.multiple_of(block * LANES, LANES), LANES), :].T
        t = t[0:32] + t[32:64] + t[64:96]
        x, v, a = (targets[block, k : k + 3, :] for k in (0, 3, 6))
        out[block, 0:3, :] = t[1:4] - x * t[0:1]
        out[block, 3:6, :] = t[4:7] - v * t[0:1] - 3.0 * (t[11:14] - x * t[10:11])
        out[block, 6:9, :] = (
            t[7:10] - a * t[0:1] - 6.0 * (t[14:17] - v * t[10:11]) + 15.0 * (t[18:21] - x * t[17:18])
        )
        return carry

    lax.fori_loop(0, target_blocks, finish, 0)


def pair_sums(targets, sources, tile_i=256, tile_j=256):
    target_count, source_count = targets.shape[0] * LANES, sources.shape[0] * LANES
    return pl.pallas_call(
        functools.partial(pair_kernel, tile_i, tile_j),
        out_shape=jax.ShapeDtypeStruct((targets.shape[0], 9, LANES), F32),
        in_specs=[pl.BlockSpec(memory_space=pltpu.VMEM)] * 2,
        out_specs=pl.BlockSpec(memory_space=pltpu.VMEM),
        scratch_shapes=[
            pltpu.VMEM((32, WIDE * LANES), F32),
            pltpu.VMEM((target_count, LANES), BF16),
            pltpu.VMEM((target_count, LANES), BF16),
            pltpu.VMEM((96, source_count), BF16),
            pltpu.VMEM((96, source_count), BF16),
            pltpu.VMEM((source_count, LANES), BF16),
            pltpu.VMEM((source_count, LANES), BF16),
            pltpu.VMEM((source_count, LANES), BF16),
            pltpu.VMEM((3, target_count, LANES), F32),
            pltpu.VMEM((target_count, LANES), F32),
        ],
        compiler_params=pltpu.CompilerParams(vmem_limit_bytes=56 * 2**20),
        name="pair_sums",
    )(targets, sources)


def gathered(block, axis):
    count = lax.axis_size(axis)
    copies = jnp.broadcast_to(block[None], (count,) + block.shape)
    return lax.all_to_all(copies, axis, 0, 0, tiled=True)


def on_device(star_phase, star_mass, due_mask):
    stars = jnp.concatenate(
        [star_phase, star_mass[None, :], jnp.zeros((6, star_mass.shape[0]), F32)], axis=0
    )
    targets = gathered(stars, "col")
    sources = gathered(stars, "row")
    sums = pair_sums(targets, sources)
    mine = jnp.sum(lax.all_to_all(sums, "col", 0, 0, tiled=True), axis=0)
    total = star_mass.shape[0] * lax.axis_size("row") * lax.axis_size("col")
    return mine / jnp.float32(total) * due_mask.astype(F32)[None, :]


def solution(mesh):
    both = ("row", "col")
    return jax.shard_map(
        on_device, mesh=mesh, in_specs=(P(None, both), P(both), P(both)), out_specs=P(None, both), check_vma=False
    )
```

time: 794 us -> 128 us (0.16)
  the two profiles are of different devices: /device:TPU:24 before, /device:TPU:1 now
where the time goes in v1:
time: 128 us
  Pallas kernels  57 us (45%)
  blocking collectives  54.2 us (42%)
  waiting for transfers between devices  8.51 us (7%)
  starting transfers between devices  5.76 us (4%)
  other arithmetic  1.4 us (1%)
    pallas_call x1, Pallas kernels, pair_sums(): pl.pallas_call(functools.partial(pair_kernel, tile_i, tile_j), out_shape=...  57 us
    all_to_all x2, blocking collectives, gathered(): return lax.all_to_all(copies, axis, 0, 0, tiled=True)  54.2 us
    all_to_all x1, waiting for transfers between devices, on_device(): mine = jnp.sum(lax.all_to_all(sums, 'col', 0, 0, tiled=True), axis=0)  8.51 us
    all_to_all x1, starting transfers between devices, on_device(): mine = jnp.sum(lax.all_to_all(sums, 'col', 0, 0, tiled=True), axis=0)  5.76 us
  transfers between devices with their start and end apart: 1, of which 1 were waited for; matrix products, arithmetic and copies ran while one was open for 0% of the time, Pallas kernels for 0%

profile of v1, /device:TPU:1, one launch (start us, length us, event | category | flops | bytes accessed | tf_op | source)
XLA Modules:
  0.0 127.7 jit_solution(425068271921081634)
XLA Ops:
  0.0 0.1 pad.2.clone
  0.1 0.0 copy-start
  0.1 0.7 copy-done
  0.7 0.8 maximum_maximum_fusion
  1.5 16.8 %all_to_all.15.targets = f32[16,16,128]{2,1,0:T(8,128)} all-to-all(f32[16,16,128]{2,1,0:T(8,128)S(1)} %broadcast_in_dim.10), channel_id=1, replica_groups=mesh['row'=32,'col'=16] {'col'}, dimensions={0} | all-to-all | bytes 262144 | tf_op jit(solution)/shard_map/all_to_all | solution.py:162
  18.3 37.4 %all_to_all.16.sources = f32[32,16,128]{2,1,0:T(8,128)} all-to-all(f32[32,16,128]{2,1,0:T(8,128)S(1)} %broadcast_in_dim.22), channel_id=1, replica_groups=mesh['row'=32,'col'=16] {'row'}, dimensions={0} | all-to-all | bytes 524288 | tf_op jit(solution)/shard_map/all_to_all | solution.py:162
  55.7 57.0 %pair_sums.1 = f32[16,9,128]{2,1,0:T(8,128)} custom-call(f32[16,16,128]{2,1,0:T(8,128)} %all_to_all.15.targets, f32[32,16,128]{2,1,0:T(8,128)} %all_to_all.16.sources), custom_call_target="tpu_custom_call" | custom-call | tf_op jit(solution)/shard_map/pair_sums/pallas_call | solution.py:137
  112.8 0.0 copy-start.1
  112.8 5.8 %all-to-all-start.2 = ((f32[16,9,128]{2,1,0:T(8,128)}), f32[16,9,128]{2,1,0:T(8,128)S(1)}, u32[]{:S(2)}, u32[]{:S(2)}) async-start(f32[16,9,128]{2,1,0:T(8,128)} %pair_sums.1), calls=%async_computation.2 | async-start | bytes 262144 | tf_op jit(solution)/shard_map/all_to_all | solution.py:172
  118.5 0.0 copy-done.1
  118.6 8.5 %all-to-all-done.2 = f32[16,9,128]{2,1,0:T(8,128)S(1)} async-done(((f32[16,9,128]{2,1,0:T(8,128)}), f32[16,9,128]{2,1,0:T(8,128)S(1)}, u32[]{:S(2)}, u32[]{:S(2)}) %all-to-all-start.2) | async-done | bytes 73760 | tf_op jit(solution)/shard_map/all_to_all | solution.py:172
  127.1 0.6 broadcast_multiply_fusion
  (5 shorter events, 0.1 us)
Async XLA Ops:
  0.1 0.7 copy-start
  112.8 5.8 %copy-start.1 = (s32[128]{0:T(128)S(1)}, s32[128]{0:T(128)}, u32[]{:S(2)}) copy-start(s32[128]{0:T(128)} %param.5) | copy-start | bytes 1540
  112.8 14.3 %all-to-all-start.2 = ((f32[16,9,128]{2,1,0:T(8,128)}), f32[16,9,128]{2,1,0:T(8,128)S(1)}, u32[]{:S(2)}, u32[]{:S(2)}) async-start(f32[16,9,128]{2,1,0:T(8,128)} %pair_sums.1), calls=%async_computation.2 | async-start | bytes 262144 | tf_op jit(solution)/shard_map/all_to_all | solution.py:172

commit v2 on v1

v2 whole, which is shorter than its diff:
```python
import functools

import jax
import jax.numpy as jnp
from jax import lax
from jax.experimental import pallas as pl
from jax.experimental.pallas import tpu as pltpu
from jax.sharding import PartitionSpec as P

F32 = jnp.float32
BF16 = jnp.bfloat16
SOFTENING = 0.01
LANES = 128
TARGET_TILE = 256
WIDE = 4
COMBOS = ("hh", "hm", "mh", "mm", "hl", "lh")


def split3(value):
    high = value.astype(BF16)
    rest = value - high.astype(F32)
    middle = rest.astype(BF16)
    low = (rest - middle.astype(F32)).astype(BF16)
    return {"h": high, "m": middle, "l": low}


def dot(left, right):
    return jnp.dot(left, right, preferred_element_type=F32)


def pair_kernel(
    tile, unroll, targets, sources, out, stage, left_rate, left_second,
    right_rate, right_second, feats, place, totals
):
    target_blocks, source_blocks = targets.shape[0], sources.shape[0]
    target_count, source_count = target_blocks * LANES, source_blocks * LANES
    width = WIDE * LANES

    def rows(ref, block, low, high):
        return jnp.concatenate([ref[block * WIDE + k, low:high, :] for k in range(WIDE)], axis=1)

    def put(pieces, height):
        stage[0:height, :] = jnp.zeros((height, width), F32)
        for at, piece in pieces:
            stage[at : at + piece.shape[0], :] = piece
        return split3(stage[0:height, :])

    one = jnp.ones((1, width), F32)

    def prepare_sources(block, carry):
        lanes = pl.ds(pl.multiple_of(block * width, width), width)
        x, v, a = (rows(sources, block, k, k + 3) for k in (0, 3, 6))
        m = rows(sources, block, 9, 10)
        x_v = jnp.sum(x * v, axis=0, keepdims=True)
        second = jnp.sum(v * v + x * a, axis=0, keepdims=True)
        empty = jnp.zeros((32, width), F32)
        for ref, pieces in (
            (right_rate, [(0, v), (3, x), (6, one), (7, x_v)]),
            (right_second, [(0, 0.2 * v), (3, 0.2 * a), (6, 0.2 * x), (9, one), (10, 0.2 * second)]),
        ):
            parts = put(pieces, 16)
            tall = jnp.concatenate([parts[c[1]].astype(F32) for c in COMBOS] + [empty], axis=0)
            ref[lanes, :] = tall.T.astype(BF16)
        for k in range(3):
            place[k, lanes, :] = jnp.broadcast_to(x[k : k + 1, :], (LANES, width)).T
        parts = put([(0, m), (1, m * x), (4, m * v), (7, m * a)], 16)
        stage[...] = jnp.zeros_like(stage)
        for k, name in enumerate("hml"):
            part = parts[name].astype(F32)
            stage[10 * k : 10 * k + 10, :] = part[0:10]
            stage[32 + 7 * k : 39 + 7 * k, :] = part[0:7]
            stage[64 + 4 * k : 68 + 4 * k, :] = part[0:4]
        feats[:, lanes] = stage[...].astype(BF16)
        return carry

    def prepare_targets(block, carry):
        lanes = pl.ds(pl.multiple_of(block * width, width), width)
        x, v, a = (rows(targets, block, k, k + 3) for k in (0, 3, 6))
        x_v = jnp.sum(x * v, axis=0, keepdims=True)
        second = jnp.sum(v * v + x * a, axis=0, keepdims=True)
        for ref, pieces in (
            (left_rate, [(0, -x), (3, -v), (6, x_v), (7, one)]),
            (left_second, [(0, -2.0 * v), (3, -x), (6, -a), (9, 0.2 * second), (10, one)]),
        ):
            parts = put(pieces, 16)
            ref[:, lanes] = jnp.concatenate([parts[c[0]] for c in COMBOS], axis=0)
        return carry

    lax.fori_loop(0, source_blocks // WIDE, prepare_sources, 0)
    lax.fori_loop(0, target_blocks // WIDE, prepare_targets, 0)
    totals[...] = jnp.zeros_like(totals)
    turns = source_count // (tile * unroll)
    tb = TARGET_TILE // LANES

    def cell(step, carry):
        i_at, j_at = step // turns, step % turns
        lanes = pl.ds(pl.multiple_of(i_at * TARGET_TILE, TARGET_TILE), TARGET_TILE)
        xs=[jnp.concatenate([targets[i_at * tb + q, k : k + 1, :] for q in range(tb)],axis=1) for k in range(3)]
        sums = [None, None, None]
        for turn in range(unroll):
            js = pl.ds(pl.multiple_of((j_at * unroll + turn) * tile, tile), tile)
            rate = dot(right_rate[js, 0:96], left_rate[:, lanes])
            second = dot(right_second[js, 0:96], left_second[:, lanes])
            spread = None
            for k in range(3):
                there = jnp.concatenate([place[k, js, :]] * tb, axis=1)
                delta = there - xs[k]
                spread = delta * delta + SOFTENING if spread is None else spread + delta * delta
            recip = lax.rsqrt(spread)
            square = recip * recip
            cube = recip * square
            p = rate * square
            weights = (cube, p * cube, (p * p - second * square) * cube)
            for k, weight in enumerate(weights):
                high = weight.astype(BF16)
                low = (weight - high.astype(F32)).astype(BF16)
                feat = feats[32 * k : min(32 * k + 32, 80), js]
                part = dot(feat, high) + dot(feat, low)
                sums[k] = part if sums[k] is None else sums[k] + part
        totals[:, lanes] += jnp.concatenate(sums, axis=0)
        return carry

    lax.fori_loop(0, (target_count // TARGET_TILE) * turns, cell, 0)

    def finish(block, carry):
        t = totals[:, pl.ds(pl.multiple_of(block * LANES, LANES), LANES)]
        c = t[0:10] + t[10:20] + t[20:30]
        p = t[32:39] + t[39:46] + t[46:53]
        u = t[64:68] + t[68:72] + t[72:76]
        x, v, a = (targets[block, k : k + 3, :] for k in (0, 3, 6))
        out[block, 0:3, :] = c[1:4] - x * c[0:1]
        out[block, 3:6, :] = c[4:7] - v * c[0:1] - 3.0 * (p[1:4] - x * p[0:1])
        out[block, 6:9, :] = (
            c[7:10] - a * c[0:1] - 6.0 * (p[4:7] - v * p[0:1]) + 15.0 * (u[1:4] - x * u[0:1])
        )
        return carry

    lax.fori_loop(0, target_blocks, finish, 0)


def pair_sums(targets, sources, tile=256, unroll=8):
    target_count, source_count = targets.shape[0] * LANES, sources.shape[0] * LANES
    return pl.pallas_call(
        functools.partial(pair_kernel, tile, unroll),
        out_shape=jax.ShapeDtypeStruct((targets.shape[0], 9, LANES), F32),
        in_specs=[pl.BlockSpec(memory_space=pltpu.VMEM)] * 2,
        out_specs=pl.BlockSpec(memory_space=pltpu.VMEM),
        scratch_shapes=[
            pltpu.VMEM((80, WIDE * LANES), F32),
            pltpu.VMEM((96, target_count), BF16),
            pltpu.VMEM((96, target_count), BF16),
            pltpu.VMEM((source_count, LANES), BF16),
            pltpu.VMEM((source_count, LANES), BF16),
            pltpu.VMEM((80, source_count), BF16),
            pltpu.VMEM((3, source_count, LANES), F32),
            pltpu.VMEM((80, target_count), F32),
        ],
        compiler_params=pltpu.CompilerParams(vmem_limit_bytes=56 * 2**20),
        name="pair_sums",
    )(targets, sources)


AXES = ("row", "col")


def device_groups(rows, cols):
    planes, lines = {}, {}
    for row in range(rows):
        for col in range(cols):
            z_hi, inner = row // 8, row % 8
            z_lo, x = col // 4, col % 4
            planes.setdefault((z_hi, z_lo), []).append(row * cols + col)
            lines.setdefault((inner, x), []).append(row * cols + col)
    return list(planes.values()), list(lines.values())


def exchange(blocks, groups):
    return lax.all_to_all(blocks, AXES, 0, 0, axis_index_groups=groups, tiled=True)


def gathered(block, groups):
    return exchange(jnp.broadcast_to(block[None], (len(groups[0]),) + block.shape), groups)


def on_device(star_phase, star_mass, due_mask):
    rows, cols = lax.axis_size("row"), lax.axis_size("col")
    planes, lines = device_groups(rows, cols)
    stars = jnp.concatenate(
        [star_phase, star_mass[None, :], jnp.zeros((6, star_mass.shape[0]), F32)], axis=0
    )
    targets = gathered(stars, planes)
    sources = gathered(stars, lines)
    sums = pair_sums(targets, sources)
    mine = jnp.sum(exchange(sums, planes), axis=0)
    total = star_mass.shape[0] * rows * cols
    return mine / jnp.float32(total) * due_mask.astype(F32)[None, :]


def solution(mesh):
    return jax.shard_map(
        on_device, mesh=mesh, in_specs=(P(None, AXES), P(AXES), P(AXES)), out_specs=P(None, AXES), check_vma=False
    )
```

time: 128 us -> 105 us (0.82)
  Pallas kernels: 57 us -> 42.6 us
  blocking collectives: 54.2 us -> 44.4 us
    pallas_call x1, Pallas kernels: 57 us -> 42.6 us  [pair_sums(): pl.pallas_call(functools.partial(pair_kernel, tile, unroll), out_shape=ja...]
    all_to_all x2, blocking collectives: 54.2 us -> 44.4 us  [exchange(): lax.all_to_all(blocks, AXES, 0, 0, axis_index_groups=groups, tiled=True)]
where the time goes in v2:
time: 105 us
  blocking collectives  44.4 us (42%)
  Pallas kernels  42.6 us (41%)
  waiting for transfers between devices  8.87 us (8%)
  starting transfers between devices  6.88 us (7%)
  other arithmetic  1.41 us (1%)
    all_to_all x2, blocking collectives, exchange(): lax.all_to_all(blocks, AXES, 0, 0, axis_index_groups=groups, tiled=True)  44.4 us
    pallas_call x1, Pallas kernels, pair_sums(): pl.pallas_call(functools.partial(pair_kernel, tile, unroll), out_shape=ja...  42.6 us
    all_to_all x1, waiting for transfers between devices, exchange(): lax.all_to_all(blocks, AXES, 0, 0, axis_index_groups=groups, tiled=True)  8.87 us
    all_to_all x1, starting transfers between devices, exchange(): lax.all_to_all(blocks, AXES, 0, 0, axis_index_groups=groups, tiled=True)  6.88 us
  transfers between devices with their start and end apart: 1, of which 1 were waited for; matrix products, arithmetic and copies ran while one was open for 0% of the time, Pallas kernels for 0%

profile of v2, /device:TPU:1, one launch (start us, length us, event | category | flops | bytes accessed | tf_op | source)
XLA Modules:
  0.0 105.0 jit_solution(10480122169180708435)
XLA Ops:
  0.0 0.1 pad.2.clone
  0.1 0.0 copy-start
  0.1 0.7 copy-done
  0.7 0.8 maximum_maximum_fusion
  1.5 19.2 %all_to_all.15.targets = f32[32,16,128]{2,1,0:T(8,128)} all-to-all(f32[32,16,128]{2,1,0:T(8,128)S(1)} %broadcast_in_dim.10), channel_id=1, replica_groups={{0,1,2,3,16,17,18,19,32,33,34,35,48,49,50,51,64,65,66,67,80,81,82,83,96..., dimensions={0} | all-to-all | bytes 524288 | tf_op jit(solution)/shard_map/all_to_all | solution.py:178
  20.7 25.2 %all_to_all.16.sources = f32[16,16,128]{2,1,0:T(8,128)} all-to-all(f32[16,16,128]{2,1,0:T(8,128)S(1)} %broadcast_in_dim.22), channel_id=1, replica_groups={{0,4,8,12,128,132,136,140,256,260,264,268,384,388,392,396},{1,5,9,13,12..., dimensions={0} | all-to-all | bytes 262144 | tf_op jit(solution)/shard_map/all_to_all | solution.py:178
  45.9 42.6 %pair_sums.1 = f32[32,9,128]{2,1,0:T(8,128)} custom-call(f32[32,16,128]{2,1,0:T(8,128)} %all_to_all.15.targets, f32[16,16,128]{2,1,0:T(8,128)} %all_to_all.16.sources), custom_call_target="tpu_custom_call" | custom-call | tf_op jit(solution)/shard_map/pair_sums/pallas_call | solution.py:143
  88.5 0.0 copy-start.1
  88.5 6.9 %all-to-all-start.2 = ((f32[32,9,128]{2,1,0:T(8,128)}), f32[32,9,128]{2,1,0:T(8,128)S(1)}, u32[]{:S(2)}, u32[]{:S(2)}) async-start(f32[32,9,128]{2,1,0:T(8,128)} %pair_sums.1), calls=%async_computation.2 | async-start | bytes 524288 | tf_op jit(solution)/shard_map/all_to_all | solution.py:178
  95.4 0.0 copy-done.1
  95.4 8.9 %all-to-all-done.2 = f32[32,9,128]{2,1,0:T(8,128)S(1)} async-done(((f32[32,9,128]{2,1,0:T(8,128)}), f32[32,9,128]{2,1,0:T(8,128)S(1)}, u32[]{:S(2)}, u32[]{:S(2)}) %all-to-all-start.2) | async-done | bytes 147488 | tf_op jit(solution)/shard_map/all_to_all | solution.py:178
  104.4 0.6 broadcast_multiply_fusion
  (5 shorter events, 0.1 us)
Async XLA Ops:
  0.1 0.7 copy-start
  88.5 6.9 %copy-start.1 = (s32[128]{0:T(128)S(1)}, s32[128]{0:T(128)}, u32[]{:S(2)}) copy-start(s32[128]{0:T(128)} %param.5) | copy-start | bytes 1540
  88.5 15.8 %all-to-all-start.2 = ((f32[32,9,128]{2,1,0:T(8,128)}), f32[32,9,128]{2,1,0:T(8,128)S(1)}, u32[]{:S(2)}, u32[]{:S(2)}) async-start(f32[32,9,128]{2,1,0:T(8,128)} %pair_sums.1), calls=%async_computation.2 | async-start | bytes 524288 | tf_op jit(solution)/shard_map/all_to_all | solution.py:178

commit v3 on v2

--- a/solution.py
+++ b/solution.py
@@ -13,6 +13,7 @@
 LANES = 128
 TARGET_TILE = 256
 WIDE = 4
+DUE = 10
 COMBOS = ("hh", "hm", "mh", "mm", "hl", "lh")
 
 
@@ -30,7 +31,7 @@
 
 def pair_kernel(
     tile, unroll, targets, sources, out, stage, left_rate, left_second,
-    right_rate, right_second, feats, place, totals
+    right_rate, right_second, feats, place, totals, due, results, offsets
 ):
     target_blocks, source_blocks = targets.shape[0], sources.shape[0]
     target_count, source_count = target_blocks * LANES, source_blocks * LANES
@@ -73,9 +74,28 @@
         feats[:, lanes] = stage[...].astype(BF16)
         return carry
 
+    lane = lax.broadcasted_iota(jnp.int32, (16, LANES), 1)
+    counts = [jnp.sum(targets[k, DUE : DUE + 1, :]).astype(jnp.int32) for k in range(target_blocks)]
+    offset = jnp.int32(0)
+    for k in range(target_blocks):
+        offsets[k] = offset
+        offset = offset + counts[k]
+    tiles = (offset + TARGET_TILE - 1) // TARGET_TILE
+    due[...] = jnp.zeros_like(due)
+    results[...] = jnp.zeros_like(results)
+
+    def gather_due(block, carry):
+        at, shift = offsets[block] // LANES, offsets[block] % LANES
+        moved = pltpu.roll(targets[block], shift, 1)
+        due[at] = jnp.where(lane >= shift, moved, due[at])
+        due[at + 1] = moved
+        return carry
+
+    lax.fori_loop(0, target_blocks, gather_due, 0)
+
     def prepare_targets(block, carry):
         lanes = pl.ds(pl.multiple_of(block * width, width), width)
-        x, v, a = (rows(targets, block, k, k + 3) for k in (0, 3, 6))
+        x, v, a = (rows(due, block, k, k + 3) for k in (0, 3, 6))
         x_v = jnp.sum(x * v, axis=0, keepdims=True)
         second = jnp.sum(v * v + x * a, axis=0, keepdims=True)
         for ref, pieces in (
@@ -87,7 +107,7 @@
         return carry
 
     lax.fori_loop(0, source_blocks // WIDE, prepare_sources, 0)
-    lax.fori_loop(0, target_blocks // WIDE, prepare_targets, 0)
+    lax.fori_loop(0, (offset + width - 1) // width, prepare_targets, 0)
     totals[...] = jnp.zeros_like(totals)
     turns = source_count // (tile * unroll)
     tb = TARGET_TILE // LANES
@@ -95,7 +115,7 @@
     def cell(step, carry):
         i_at, j_at = step // turns, step % turns
         lanes = pl.ds(pl.multiple_of(i_at * TARGET_TILE, TARGET_TILE), TARGET_TILE)
-        xs=[jnp.concatenate([targets[i_at * tb + q, k : k + 1, :] for q in range(tb)],axis=1) for k in range(3)]
+        xs=[jnp.concatenate([due[i_at * tb + q, k : k + 1, :] for q in range(tb)],axis=1) for k in range(3)]
         sums = [None, None, None]
         for turn in range(unroll):
             js = pl.ds(pl.multiple_of((j_at * unroll + turn) * tile, tile), tile)
@@ -120,22 +140,30 @@
         totals[:, lanes] += jnp.concatenate(sums, axis=0)
         return carry
 
-    lax.fori_loop(0, (target_count // TARGET_TILE) * turns, cell, 0)
+    lax.fori_loop(0, tiles * turns, cell, 0)
 
     def finish(block, carry):
         t = totals[:, pl.ds(pl.multiple_of(block * LANES, LANES), LANES)]
         c = t[0:10] + t[10:20] + t[20:30]
         p = t[32:39] + t[39:46] + t[46:53]
         u = t[64:68] + t[68:72] + t[72:76]
-        x, v, a = (targets[block, k : k + 3, :] for k in (0, 3, 6))
-        out[block, 0:3, :] = c[1:4] - x * c[0:1]
-        out[block, 3:6, :] = c[4:7] - v * c[0:1] - 3.0 * (p[1:4] - x * p[0:1])
-        out[block, 6:9, :] = (
+        x, v, a = (due[block, k : k + 3, :] for k in (0, 3, 6))
+        results[block, 0:3, :] = c[1:4] - x * c[0:1]
+        results[block, 3:6, :] = c[4:7] - v * c[0:1] - 3.0 * (p[1:4] - x * p[0:1])
+        results[block, 6:9, :] = (
             c[7:10] - a * c[0:1] - 6.0 * (p[4:7] - v * p[0:1]) + 15.0 * (u[1:4] - x * u[0:1])
         )
         return carry
 
-    lax.fori_loop(0, target_blocks, finish, 0)
+    lax.fori_loop(0, tiles * tb, finish, 0)
+
+    def return_due(block, carry):
+        at, shift = offsets[block] // LANES, offsets[block] % LANES
+        both = jnp.where(lane >= shift, results[at], results[at + 1])
+        out[block] = pltpu.roll(both, (LANES - shift) % LANES, 1)[0:9]
+        return carry
+
+    lax.fori_loop(0, target_blocks, return_due, 0)
 
 
 def pair_sums(targets, sources, tile=256, unroll=8):
@@ -154,10 +182,61 @@
             pltpu.VMEM((80, source_count), BF16),
             pltpu.VMEM((3, source_count, LANES), F32),
             pltpu.VMEM((80, target_count), F32),
+            pltpu.VMEM((targets.shape[0] + 2, 16, LANES), F32),
+            pltpu.VMEM((targets.shape[0] + 2, 16, LANES), F32),
+            pltpu.SMEM((targets.shape[0],), jnp.int32),
         ],
         compiler_params=pltpu.CompilerParams(vmem_limit_bytes=56 * 2**20),
         name="pair_sums",
     )(targets, sources)
+
+
+def due_first(mask):
+    row = lax.broadcasted_iota(jnp.int32, (LANES, LANES), 0)
+    star = lax.broadcasted_iota(jnp.int32, (LANES, LANES), 1)
+    ones = jnp.broadcast_to(mask.astype(F32), (16, LANES)).astype(BF16)
+    rank = dot(ones, jnp.where(row <= star, 1.0, 0.0).astype(BF16))[0:1]
+    count = rank[:, LANES - 1 : LANES]
+    index = star[0:1].astype(F32)
+    to = jnp.where(mask > 0, rank - 1.0, count + index - rank)
+    return jnp.where(jnp.broadcast_to(to, (LANES, LANES)) == row.astype(F32), 1.0, 0.0).astype(BF16)
+
+
+def moved(value, order, dims):
+    parts = split3(value)
+    h, m, l = (
+        lax.dot_general(parts[k], order, (dims, ((), ())), preferred_element_type=F32) for k in "hml"
+    )
+    return (h + m) + l
+
+
+def pack_kernel(phase, mass, mask, plane, line, stage):
+    stage[...] = jnp.zeros_like(stage)
+    stage[0:9, :] = phase[...]
+    stage[9:10, :] = mass[...]
+    stage[DUE : DUE + 1, :] = mask[...].astype(F32)
+    packed = moved(stage[...], due_first(mask[...]), ((1,), (1,)))
+    plane[...] = jnp.broadcast_to(packed[None], plane.shape)
+    line[...] = jnp.broadcast_to(packed[None], line.shape)
+
+
+def unpack_kernel(scale, sums, mask, out, stage):
+    stage[...] = jnp.zeros_like(stage)
+    stage[0:9, :] = jnp.sum(sums[...], axis=0)
+    back = moved(stage[...], due_first(mask[...]), ((1,), (0,)))
+    out[...] = back[0:9] * scale * mask[...].astype(F32)
+
+
+def small_call(kernel, shapes, name, *args):
+    vmem = pl.BlockSpec(memory_space=pltpu.VMEM)
+    return pl.pallas_call(
+        kernel,
+        out_shape=tuple(jax.ShapeDtypeStruct(shape, F32) for shape in shapes),
+        in_specs=[vmem] * len(args),
+        out_specs=(vmem,) * len(shapes),
+        scratch_shapes=[pltpu.VMEM((16, LANES), F32)],
+        name=name,
+    )(*args)
 
 
 AXES = ("row", "col")
@@ -178,22 +257,18 @@
     return lax.all_to_all(blocks, AXES, 0, 0, axis_index_groups=groups, tiled=True)
 
 
-def gathered(block, groups):
-    return exchange(jnp.broadcast_to(block[None], (len(groups[0]),) + block.shape), groups)
-
-
 def on_device(star_phase, star_mass, due_mask):
     rows, cols = lax.axis_size("row"), lax.axis_size("col")
     planes, lines = device_groups(rows, cols)
-    stars = jnp.concatenate(
-        [star_phase, star_mass[None, :], jnp.zeros((6, star_mass.shape[0]), F32)], axis=0
-    )
-    targets = gathered(stars, planes)
-    sources = gathered(stars, lines)
-    sums = pair_sums(targets, sources)
-    mine = jnp.sum(exchange(sums, planes), axis=0)
-    total = star_mass.shape[0] * rows * cols
-    return mine / jnp.float32(total) * due_mask.astype(F32)[None, :]
+    mass, mask = star_mass[None, :], due_mask[None, :]
+    shapes = [(len(groups[0]), 16, LANES) for groups in (planes, lines)]
+    for_plane, for_line = small_call(pack_kernel, shapes, "pack_stars", star_phase, mass, mask)
+    targets = exchange(for_plane, planes)
+    sources = exchange(for_line, lines)
+    sums = exchange(pair_sums(targets, sources), planes)
+    scale = 1.0 / (LANES * rows * cols)
+    kernel = functools.partial(unpack_kernel, scale)
+    return small_call(kernel, [star_phase.shape], "unpack_sums", sums, mask)[0]
 
 
 def solution(mesh):

time: 105 us -> 103 us (0.981)
  blocking collectives: 44.4 us -> 60.5 us
  waiting for transfers between devices: 8.87 us -> 0 us
  starting transfers between devices: 6.88 us -> 0 us
  other arithmetic: 1.41 us -> 0 us
  Pallas kernels: 42.6 us -> 41.4 us
    all_to_all x2 -> x3, blocking collectives: 44.4 us -> 60.5 us  [exchange(): lax.all_to_all(blocks, AXES, 0, 0, axis_index_groups=groups, tiled=True)]
    all_to_all x1 -> x0, waiting for transfers between devices: 8.87 us -> none  [exchange(): lax.all_to_all(blocks, AXES, 0, 0, axis_index_groups=groups, tiled=True)]
    all_to_all x1 -> x0, starting transfers between devices: 6.88 us -> none  [exchange(): lax.all_to_all(blocks, AXES, 0, 0, axis_index_groups=groups, tiled=True)]
    pallas_call x1, Pallas kernels: 42.6 us -> 37.6 us  [pair_sums(): pl.pallas_call(functools.partial(pair_kernel, tile, unroll), out_shape=ja...]
    pallas_call x0 -> x2, Pallas kernels: none -> 3.78 us  [small_call(): pl.pallas_call(kernel, out_shape=tuple((jax.ShapeDtypeStruct(shape, F32)...]
  transfers between devices with their start and end apart: 1 -> 0, of which waited for: 1 -> 0; matrix products, arithmetic and copies ran while one was open for 0% -> 0% of each run, Pallas kernels for 0% -> 0%
where the time goes in v3:
time: 103 us; the launch traced here: 102 us
  blocking collectives  60.5 us (59%)
  Pallas kernels  41.4 us (40%)
    all_to_all x3, blocking collectives, exchange(): lax.all_to_all(blocks, AXES, 0, 0, axis_index_groups=groups, tiled=True)  60.5 us
    pallas_call x1, Pallas kernels, pair_sums(): pl.pallas_call(functools.partial(pair_kernel, tile, unroll), out_shape=ja...  37.6 us
    pallas_call x2, Pallas kernels, small_call(): pl.pallas_call(kernel, out_shape=tuple((jax.ShapeDtypeStruct(shape, F32)...  3.78 us

profile of v3, /device:TPU:1, one launch (start us, length us, event | category | flops | bytes accessed | tf_op | source)
XLA Modules:
  0.0 102.0 jit_solution(13101898426737343087)
XLA Ops:
  0.0 1.9 %pack_stars.1 = (f32[32,16,128]{2,1,0:T(8,128)}, f32[16,16,128]{2,1,0:T(8,128)}) custom-call(f32[9,128]{1,0:T(8,128)} %phase.1, f32[1,128]{1,0:T(1,128)} %bitcast.4, s32[1,128]{1,0:T(1,128)} %bitcast.2), custom_call_target="tpu_custom_call" | custom-call | tf_op jit(solution)/shard_map/pack_stars/pallas_call | solution.py:232
  1.9 0.0 copy-start
  1.9 20.2 %all_to_all.15.targets = f32[32,16,128]{2,1,0:T(8,128)} all-to-all(f32[32,16,128]{2,1,0:T(8,128)} %get-tuple-element.7), channel_id=1, replica_groups={{0,1,2,3,16,17,18,19,32,33,34,35,48,49,50,51,64,65,66,67,80,81,82,83,96..., dimensions={0} | all-to-all | bytes 524288 | tf_op jit(solution)/shard_map/all_to_all | solution.py:257
  22.1 0.0 copy-done
  22.1 24.5 %all_to_all.16.sources = f32[16,16,128]{2,1,0:T(8,128)} all-to-all(f32[16,16,128]{2,1,0:T(8,128)S(1)} %copy-done), channel_id=1, replica_groups={{0,4,8,12,128,132,136,140,256,260,264,268,384,388,392,396},{1,5,9,13,12..., dimensions={0} | all-to-all | bytes 262144 | tf_op jit(solution)/shard_map/all_to_all | solution.py:257
  46.6 37.6 %pair_sums.1 = f32[32,9,128]{2,1,0:T(8,128)} custom-call(f32[32,16,128]{2,1,0:T(8,128)} %all_to_all.15.targets, f32[16,16,128]{2,1,0:T(8,128)} %all_to_all.16.sources), custom_call_target="tpu_custom_call" | custom-call | tf_op jit(solution)/shard_map/pair_sums/pallas_call | solution.py:171
  84.2 15.9 %all_to_all.17.sums = f32[32,9,128]{2,1,0:T(8,128)} all-to-all(f32[32,9,128]{2,1,0:T(8,128)} %pair_sums.1), channel_id=1, replica_groups={{0,1,2,3,16,17,18,19,32,33,34,35,48,49,50,51,64,65,66,67,80,81,82,83,96..., dimensions={0} | all-to-all | bytes 294912 | tf_op jit(solution)/shard_map/all_to_all | solution.py:257
  100.1 1.9 %unpack_sums.1 = f32[9,128]{1,0:T(8,128)} custom-call(f32[32,9,128]{2,1,0:T(8,128)} %all_to_all.17.sums, s32[1,128]{1,0:T(1,128)} %bitcast.3), custom_call_target="tpu_custom_call" | custom-call | tf_op jit(solution)/shard_map/unpack_sums/pallas_call | solution.py:232
Async XLA Ops:
  1.9 20.2 %copy-start = (f32[16,16,128]{2,1,0:T(8,128)S(1)}, f32[16,16,128]{2,1,0:T(8,128)}, u32[]{:S(2)}) copy-start(f32[16,16,128]{2,1,0:T(8,128)} %get-tuple-element.8) | copy-start | bytes 393220

commit v4 on v3

--- a/solution.py
+++ b/solution.py
@@ -31,7 +31,7 @@
 
 def pair_kernel(
     tile, unroll, targets, sources, out, stage, left_rate, left_second,
-    right_rate, right_second, feats, place, totals, due, results, offsets
+    right_rate, right_second, feats, place, totals, due, results
 ):
     target_blocks, source_blocks = targets.shape[0], sources.shape[0]
     target_count, source_count = target_blocks * LANES, source_blocks * LANES
@@ -76,22 +76,22 @@
 
     lane = lax.broadcasted_iota(jnp.int32, (16, LANES), 1)
     counts = [jnp.sum(targets[k, DUE : DUE + 1, :]).astype(jnp.int32) for k in range(target_blocks)]
-    offset = jnp.int32(0)
-    for k in range(target_blocks):
-        offsets[k] = offset
-        offset = offset + counts[k]
-    tiles = (offset + TARGET_TILE - 1) // TARGET_TILE
+    starts, offset = [], jnp.int32(0)
+    for count in counts:
+        starts.append(offset)
+        offset = offset + count
+    pairs_of_blocks = (offset + LANES - 1) // TARGET_TILE
+    odd_block = (offset + LANES - 1) // LANES - 2 * pairs_of_blocks
     due[...] = jnp.zeros_like(due)
     results[...] = jnp.zeros_like(results)
 
-    def gather_due(block, carry):
-        at, shift = offsets[block] // LANES, offsets[block] % LANES
-        moved = pltpu.roll(targets[block], shift, 1)
-        due[at] = jnp.where(lane >= shift, moved, due[at])
-        due[at + 1] = moved
-        return carry
-
-    lax.fori_loop(0, target_blocks, gather_due, 0)
+    placed = []
+    for k in range(target_blocks):
+        at, shift = starts[k] >> 7, starts[k] & (LANES - 1)
+        placed.append((at, shift))
+        moved_block = pltpu.roll(targets[k], shift, 1)
+        due[at] = jnp.where(lane >= shift, moved_block, due[at])
+        due[at + 1] = moved_block
 
     def prepare_targets(block, carry):
         lanes = pl.ds(pl.multiple_of(block * width, width), width)
@@ -110,12 +110,13 @@
     lax.fori_loop(0, (offset + width - 1) // width, prepare_targets, 0)
     totals[...] = jnp.zeros_like(totals)
     turns = source_count // (tile * unroll)
-    tb = TARGET_TILE // LANES
-
-    def cell(step, carry):
-        i_at, j_at = step // turns, step % turns
-        lanes = pl.ds(pl.multiple_of(i_at * TARGET_TILE, TARGET_TILE), TARGET_TILE)
-        xs=[jnp.concatenate([due[i_at * tb + q, k : k + 1, :] for q in range(tb)],axis=1) for k in range(3)]
+
+    def cell(first, tb, j_at):
+        lanes = pl.ds(pl.multiple_of(first * LANES, LANES), tb * LANES)
+        xs = [
+            jnp.concatenate([due[first + q, k : k + 1, :] for q in range(tb)], axis=1)
+            for k in range(3)
+        ]
         sums = [None, None, None]
         for turn in range(unroll):
             js = pl.ds(pl.multiple_of((j_at * unroll + turn) * tile, tile), tile)
@@ -138,9 +139,17 @@
                 part = dot(feat, high) + dot(feat, low)
                 sums[k] = part if sums[k] is None else sums[k] + part
         totals[:, lanes] += jnp.concatenate(sums, axis=0)
-        return carry
-
-    lax.fori_loop(0, tiles * turns, cell, 0)
+
+    def wide_cell(step, carry):
+        cell(step // turns * 2, 2, step % turns)
+        return carry
+
+    def narrow_cell(step, carry):
+        cell(pairs_of_blocks * 2, 1, step)
+        return carry
+
+    lax.fori_loop(0, pairs_of_blocks * turns, wide_cell, 0)
+    lax.fori_loop(0, odd_block * turns, narrow_cell, 0)
 
     def finish(block, carry):
         t = totals[:, pl.ds(pl.multiple_of(block * LANES, LANES), LANES)]
@@ -155,15 +164,11 @@
         )
         return carry
 
-    lax.fori_loop(0, tiles * tb, finish, 0)
-
-    def return_due(block, carry):
-        at, shift = offsets[block] // LANES, offsets[block] % LANES
+    lax.fori_loop(0, pairs_of_blocks * 2 + odd_block, finish, 0)
+
+    for k, (at, shift) in enumerate(placed):
         both = jnp.where(lane >= shift, results[at], results[at + 1])
-        out[block] = pltpu.roll(both, (LANES - shift) % LANES, 1)[0:9]
-        return carry
-
-    lax.fori_loop(0, target_blocks, return_due, 0)
+        out[k] = pltpu.roll(both, (LANES - shift) & (LANES - 1), 1)[0:9]
 
 
 def pair_sums(targets, sources, tile=256, unroll=8):
@@ -184,7 +189,6 @@
             pltpu.VMEM((80, target_count), F32),
             pltpu.VMEM((targets.shape[0] + 2, 16, LANES), F32),
             pltpu.VMEM((targets.shape[0] + 2, 16, LANES), F32),
-            pltpu.SMEM((targets.shape[0],), jnp.int32),
         ],
         compiler_params=pltpu.CompilerParams(vmem_limit_bytes=56 * 2**20),
         name="pair_sums",

time: 103 us -> 98.2 us (0.953)
  Pallas kernels: 41.4 us -> 37.2 us
    pallas_call x1, Pallas kernels: 37.6 us -> 33.4 us  [pair_sums(): pl.pallas_call(functools.partial(pair_kernel, tile, unroll), out_shape=ja...]
where the time goes in v4:
time: 98.2 us; the launch traced here: 97.7 us
  blocking collectives  60.5 us (62%)
  Pallas kernels  37.2 us (38%)
    all_to_all x3, blocking collectives, exchange(): lax.all_to_all(blocks, AXES, 0, 0, axis_index_groups=groups, tiled=True)  60.5 us
    pallas_call x1, Pallas kernels, pair_sums(): pl.pallas_call(functools.partial(pair_kernel, tile, unroll), out_shape=ja...  33.4 us
    pallas_call x2, Pallas kernels, small_call(): pl.pallas_call(kernel, out_shape=tuple((jax.ShapeDtypeStruct(shape, F32)...  3.78 us

profile of v4, /device:TPU:1, one launch (start us, length us, event | category | flops | bytes accessed | tf_op | source)
XLA Modules:
  0.0 97.7 jit_solution(5712160780235594204)
XLA Ops:
  0.0 1.9 %pack_stars.1 = (f32[32,16,128]{2,1,0:T(8,128)}, f32[16,16,128]{2,1,0:T(8,128)}) custom-call(f32[9,128]{1,0:T(8,128)} %phase.1, f32[1,128]{1,0:T(1,128)} %bitcast.4, s32[1,128]{1,0:T(1,128)} %bitcast.2), custom_call_target="tpu_custom_call" | custom-call | tf_op jit(solution)/shard_map/pack_stars/pallas_call | solution.py:236
  1.9 0.0 copy-start
  1.9 20.2 %all_to_all.15.targets = f32[32,16,128]{2,1,0:T(8,128)} all-to-all(f32[32,16,128]{2,1,0:T(8,128)} %get-tuple-element.7), channel_id=1, replica_groups={{0,1,2,3,16,17,18,19,32,33,34,35,48,49,50,51,64,65,66,67,80,81,82,83,96..., dimensions={0} | all-to-all | bytes 524288 | tf_op jit(solution)/shard_map/all_to_all | solution.py:261
  22.1 0.0 copy-done
  22.1 24.5 %all_to_all.16.sources = f32[16,16,128]{2,1,0:T(8,128)} all-to-all(f32[16,16,128]{2,1,0:T(8,128)S(1)} %copy-done), channel_id=1, replica_groups={{0,4,8,12,128,132,136,140,256,260,264,268,384,388,392,396},{1,5,9,13,12..., dimensions={0} | all-to-all | bytes 262144 | tf_op jit(solution)/shard_map/all_to_all | solution.py:261
  46.6 33.4 %pair_sums.1 = f32[32,9,128]{2,1,0:T(8,128)} custom-call(f32[32,16,128]{2,1,0:T(8,128)} %all_to_all.15.targets, f32[16,16,128]{2,1,0:T(8,128)} %all_to_all.16.sources), custom_call_target="tpu_custom_call" | custom-call | tf_op jit(solution)/shard_map/pair_sums/pallas_call | solution.py:176
  80.0 15.9 %all_to_all.17.sums = f32[32,9,128]{2,1,0:T(8,128)} all-to-all(f32[32,9,128]{2,1,0:T(8,128)} %pair_sums.1), channel_id=1, replica_groups={{0,1,2,3,16,17,18,19,32,33,34,35,48,49,50,51,64,65,66,67,80,81,82,83,96..., dimensions={0} | all-to-all | bytes 294912 | tf_op jit(solution)/shard_map/all_to_all | solution.py:261
  95.8 1.9 %unpack_sums.1 = f32[9,128]{1,0:T(8,128)} custom-call(f32[32,9,128]{2,1,0:T(8,128)} %all_to_all.17.sums, s32[1,128]{1,0:T(1,128)} %bitcast.3), custom_call_target="tpu_custom_call" | custom-call | tf_op jit(solution)/shard_map/unpack_sums/pallas_call | solution.py:236
Async XLA Ops:
  1.9 20.2 %copy-start = (f32[16,16,128]{2,1,0:T(8,128)S(1)}, f32[16,16,128]{2,1,0:T(8,128)}, u32[]{:S(2)}) copy-start(f32[16,16,128]{2,1,0:T(8,128)} %get-tuple-element.8) | copy-start | bytes 393220

commit v5 on v4

--- a/solution.py
+++ b/solution.py
@@ -29,29 +29,70 @@
     return jnp.dot(left, right, preferred_element_type=F32)
 
 
+def rows_of(ref, block, low, high):
+    return jnp.concatenate([ref[block * WIDE + k, low:high, :] for k in range(WIDE)], axis=1)
+
+
+def staged(stage, pieces, height):
+    stage[0:height, :] = jnp.zeros((height, stage.shape[1]), F32)
+    for at, piece in pieces:
+        stage[at : at + piece.shape[0], :] = piece
+    return split3(stage[0:height, :])
+
+
+def target_kernel(targets, due, left_rate, left_second, starts, stage):
+    width = WIDE * LANES
+    one = jnp.ones((1, width), F32)
+    target_blocks = targets.shape[0]
+    lane = lax.broadcasted_iota(jnp.int32, (16, LANES), 1)
+    counts = [jnp.sum(targets[k, DUE : DUE + 1, :]).astype(jnp.int32) for k in range(target_blocks)]
+    offset, begins = jnp.int32(0), []
+    for k, count in enumerate(counts):
+        begins.append(offset)
+        starts[k] = offset
+        offset = offset + count
+    starts[target_blocks] = offset
+    due[...] = jnp.zeros_like(due)
+
+    for k in range(target_blocks):
+        at, shift = begins[k] >> 7, begins[k] & (LANES - 1)
+        moved_block = pltpu.roll(targets[k], shift, 1)
+        due[at] = jnp.where(lane >= shift, moved_block, due[at])
+        due[at + 1] = moved_block
+
+    def prepare_targets(block, carry):
+        lanes = pl.ds(pl.multiple_of(block * width, width), width)
+        x, v, a = (rows_of(due, block, k, k + 3) for k in (0, 3, 6))
+        x_v = jnp.sum(x * v, axis=0, keepdims=True)
+        second = jnp.sum(v * v + x * a, axis=0, keepdims=True)
+        for ref, pieces in (
+            (left_rate, [(0, -x), (3, -v), (6, x_v), (7, one)]),
+            (left_second, [(0, -2.0 * v), (3, -x), (6, -a), (9, 0.2 * second), (10, one)]),
+        ):
+            parts = staged(stage, pieces, 16)
+            ref[:, lanes] = jnp.concatenate([parts[c[0]] for c in COMBOS], axis=0)
+        return carry
+
+    lax.fori_loop(0, (offset + width - 1) // width, prepare_targets, 0)
+
+
 def pair_kernel(
-    tile, unroll, targets, sources, out, stage, left_rate, left_second,
-    right_rate, right_second, feats, place, totals, due, results
+    tile, unroll, due, left_rate, left_second, starts, sources, out, stage,
+    right_rate, right_second, feats, place, totals, results
 ):
-    target_blocks, source_blocks = targets.shape[0], sources.shape[0]
-    target_count, source_count = target_blocks * LANES, source_blocks * LANES
+    target_blocks, source_blocks = out.shape[0], sources.shape[0]
+    source_count = source_blocks * LANES
     width = WIDE * LANES
-
-    def rows(ref, block, low, high):
-        return jnp.concatenate([ref[block * WIDE + k, low:high, :] for k in range(WIDE)], axis=1)
-
-    def put(pieces, height):
-        stage[0:height, :] = jnp.zeros((height, width), F32)
-        for at, piece in pieces:
-            stage[at : at + piece.shape[0], :] = piece
-        return split3(stage[0:height, :])
-
+    total = starts[target_blocks]
+    pairs_of_blocks = (total + LANES - 1) // TARGET_TILE
+    odd_block = (total + LANES - 1) // LANES - 2 * pairs_of_blocks
+    results[...] = jnp.zeros_like(results)
     one = jnp.ones((1, width), F32)
 
     def prepare_sources(block, carry):
         lanes = pl.ds(pl.multiple_of(block * width, width), width)
-        x, v, a = (rows(sources, block, k, k + 3) for k in (0, 3, 6))
-        m = rows(sources, block, 9, 10)
+        x, v, a = (rows_of(sources, block, k, k + 3) for k in (0, 3, 6))
+        m = rows_of(sources, block, 9, 10)
         x_v = jnp.sum(x * v, axis=0, keepdims=True)
         second = jnp.sum(v * v + x * a, axis=0, keepdims=True)
         empty = jnp.zeros((32, width), F32)
@@ -59,12 +100,12 @@
             (right_rate, [(0, v), (3, x), (6, one), (7, x_v)]),
             (right_second, [(0, 0.2 * v), (3, 0.2 * a), (6, 0.2 * x), (9, one), (10, 0.2 * second)]),
         ):
-            parts = put(pieces, 16)
+            parts = staged(stage, pieces, 16)
             tall = jnp.concatenate([parts[c[1]].astype(F32) for c in COMBOS] + [empty], axis=0)
             ref[lanes, :] = tall.T.astype(BF16)
         for k in range(3):
             place[k, lanes, :] = jnp.broadcast_to(x[k : k + 1, :], (LANES, width)).T
-        parts = put([(0, m), (1, m * x), (4, m * v), (7, m * a)], 16)
+        parts = staged(stage, [(0, m), (1, m * x), (4, m * v), (7, m * a)], 16)
         stage[...] = jnp.zeros_like(stage)
         for k, name in enumerate("hml"):
             part = parts[name].astype(F32)
@@ -74,40 +115,7 @@
         feats[:, lanes] = stage[...].astype(BF16)
         return carry
 
-    lane = lax.broadcasted_iota(jnp.int32, (16, LANES), 1)
-    counts = [jnp.sum(targets[k, DUE : DUE + 1, :]).astype(jnp.int32) for k in range(target_blocks)]
-    starts, offset = [], jnp.int32(0)
-    for count in counts:
-        starts.append(offset)
-        offset = offset + count
-    pairs_of_blocks = (offset + LANES - 1) // TARGET_TILE
-    odd_block = (offset + LANES - 1) // LANES - 2 * pairs_of_blocks
-    due[...] = jnp.zeros_like(due)
-    results[...] = jnp.zeros_like(results)
-
-    placed = []
-    for k in range(target_blocks):
-        at, shift = starts[k] >> 7, starts[k] & (LANES - 1)
-        placed.append((at, shift))
-        moved_block = pltpu.roll(targets[k], shift, 1)
-        due[at] = jnp.where(lane >= shift, moved_block, due[at])
-        due[at + 1] = moved_block
-
-    def prepare_targets(block, carry):
-        lanes = pl.ds(pl.multiple_of(block * width, width), width)
-        x, v, a = (rows(due, block, k, k + 3) for k in (0, 3, 6))
-        x_v = jnp.sum(x * v, axis=0, keepdims=True)
-        second = jnp.sum(v * v + x * a, axis=0, keepdims=True)
-        for ref, pieces in (
-            (left_rate, [(0, -x), (3, -v), (6, x_v), (7, one)]),
-            (left_second, [(0, -2.0 * v), (3, -x), (6, -a), (9, 0.2 * second), (10, one)]),
-        ):
-            parts = put(pieces, 16)
-            ref[:, lanes] = jnp.concatenate([parts[c[0]] for c in COMBOS], axis=0)
-        return carry
-
     lax.fori_loop(0, source_blocks // WIDE, prepare_sources, 0)
-    lax.fori_loop(0, (offset + width - 1) // width, prepare_targets, 0)
     totals[...] = jnp.zeros_like(totals)
     turns = source_count // (tile * unroll)
 
@@ -166,33 +174,53 @@
 
     lax.fori_loop(0, pairs_of_blocks * 2 + odd_block, finish, 0)
 
-    for k, (at, shift) in enumerate(placed):
+    lane = lax.broadcasted_iota(jnp.int32, (16, LANES), 1)
+    for k in range(target_blocks):
+        at, shift = starts[k] >> 7, starts[k] & (LANES - 1)
         both = jnp.where(lane >= shift, results[at], results[at + 1])
         out[k] = pltpu.roll(both, (LANES - shift) & (LANES - 1), 1)[0:9]
 
 
-def pair_sums(targets, sources, tile=256, unroll=8):
-    target_count, source_count = targets.shape[0] * LANES, sources.shape[0] * LANES
+def prepared_targets(targets):
+    blocks = targets.shape[0]
+    in_vmem = pl.BlockSpec(memory_space=pltpu.VMEM)
+    return pl.pallas_call(
+        target_kernel,
+        out_shape=(
+            jax.ShapeDtypeStruct((blocks + 2, 16, LANES), F32),
+            jax.ShapeDtypeStruct((96, blocks * LANES), BF16),
+            jax.ShapeDtypeStruct((96, blocks * LANES), BF16),
+            jax.ShapeDtypeStruct((blocks + 1,), jnp.int32),
+        ),
+        in_specs=[in_vmem],
+        out_specs=(in_vmem, in_vmem, in_vmem, pl.BlockSpec(memory_space=pltpu.SMEM)),
+        scratch_shapes=[pltpu.VMEM((16, WIDE * LANES), F32)],
+        compiler_params=pltpu.CompilerParams(vmem_limit_bytes=16 * 2**20),
+        name="prepare_targets",
+    )(targets)
+
+
+def pair_sums(prepared, sources, tile=256, unroll=8):
+    target_count, source_count = prepared[1].shape[1], sources.shape[0] * LANES
+    target_blocks = target_count // LANES
+    in_vmem = pl.BlockSpec(memory_space=pltpu.VMEM)
     return pl.pallas_call(
         functools.partial(pair_kernel, tile, unroll),
-        out_shape=jax.ShapeDtypeStruct((targets.shape[0], 9, LANES), F32),
-        in_specs=[pl.BlockSpec(memory_space=pltpu.VMEM)] * 2,
-        out_specs=pl.BlockSpec(memory_space=pltpu.VMEM),
+        out_shape=jax.ShapeDtypeStruct((target_blocks, 9, LANES), F32),
+        in_specs=[in_vmem] * 3 + [pl.BlockSpec(memory_space=pltpu.SMEM), in_vmem],
+        out_specs=in_vmem,
         scratch_shapes=[
             pltpu.VMEM((80, WIDE * LANES), F32),
-            pltpu.VMEM((96, target_count), BF16),
-            pltpu.VMEM((96, target_count), BF16),
             pltpu.VMEM((source_count, LANES), BF16),
             pltpu.VMEM((source_count, LANES), BF16),
             pltpu.VMEM((80, source_count), BF16),
             pltpu.VMEM((3, source_count, LANES), F32),
             pltpu.VMEM((80, target_count), F32),
-            pltpu.VMEM((targets.shape[0] + 2, 16, LANES), F32),
-            pltpu.VMEM((targets.shape[0] + 2, 16, LANES), F32),
+            pltpu.VMEM((target_blocks + 2, 16, LANES), F32),
         ],
-        compiler_params=pltpu.CompilerParams(vmem_limit_bytes=56 * 2**20),
+        compiler_params=pltpu.CompilerParams(vmem_limit_bytes=24 * 2**20),
         name="pair_sums",
-    )(targets, sources)
+    )(*prepared, sources)
 
 
 def due_first(mask):
@@ -214,14 +242,13 @@
     return (h + m) + l
 
 
-def pack_kernel(phase, mass, mask, plane, line, stage):
+def pack_kernel(phase, mass, mask, copies, stage):
     stage[...] = jnp.zeros_like(stage)
     stage[0:9, :] = phase[...]
     stage[9:10, :] = mass[...]
     stage[DUE : DUE + 1, :] = mask[...].astype(F32)
     packed = moved(stage[...], due_first(mask[...]), ((1,), (1,)))
-    plane[...] = jnp.broadcast_to(packed[None], plane.shape)
-    line[...] = jnp.broadcast_to(packed[None], line.shape)
+    copies[...] = jnp.broadcast_to(packed[None], copies.shape)
 
 
 def unpack_kernel(scale, sums, mask, out, stage):
@@ -265,11 +292,13 @@
     rows, cols = lax.axis_size("row"), lax.axis_size("col")
     planes, lines = device_groups(rows, cols)
     mass, mask = star_mass[None, :], due_mask[None, :]
-    shapes = [(len(groups[0]), 16, LANES) for groups in (planes, lines)]
-    for_plane, for_line = small_call(pack_kernel, shapes, "pack_stars", star_phase, mass, mask)
-    targets = exchange(for_plane, planes)
-    sources = exchange(for_line, lines)
-    sums = exchange(pair_sums(targets, sources), planes)
+    packed = [
+        small_call(pack_kernel, [(len(groups[0]), 16, LANES)], name, star_phase, mass, mask)[0]
+        for groups, name in ((planes, "pack_plane"), (lines, "pack_line"))
+    ]
+    targets = exchange(packed[0], planes)
+    sources = exchange(packed[1], lines)
+    sums = exchange(pair_sums(prepared_targets(targets), sources), planes)
     scale = 1.0 / (LANES * rows * cols)
     kernel = functools.partial(unpack_kernel, scale)
     return small_call(kernel, [star_phase.shape], "unpack_sums", sums, mask)[0]

time: 98.2 us -> 97.4 us (level)
  blocking collectives: 60.5 us -> 15.5 us
  starting transfers between devices: 0 us -> 23.4 us
  waiting for transfers between devices: 0 us -> 18 us
  Pallas kernels: 37.2 us -> 40.1 us
    all_to_all x3 -> x1, blocking collectives: 60.5 us -> 15.5 us  [exchange(): lax.all_to_all(blocks, AXES, 0, 0, axis_index_groups=groups, tiled=True)]
    all_to_all x0 -> x2, starting transfers between devices: none -> 23.4 us  [exchange(): lax.all_to_all(blocks, AXES, 0, 0, axis_index_groups=groups, tiled=True)]
    all_to_all x0 -> x2, waiting for transfers between devices: none -> 18 us  [exchange(): lax.all_to_all(blocks, AXES, 0, 0, axis_index_groups=groups, tiled=True)]
    pallas_call x2 -> x3, Pallas kernels: 3.78 us -> 5.47 us  [small_call(): pl.pallas_call(kernel, out_shape=tuple((jax.ShapeDtypeStruct(shape, F32)...]
    pallas_call x0 -> x1, Pallas kernels: none -> 1.4 us  [prepared_targets(): pl.pallas_call(target_kernel, out_shape=(jax.ShapeDtypeStruct((blocks + 2...]
  transfers between devices with their start and end apart: 0 -> 2, of which waited for: 0 -> 2; matrix products, arithmetic and copies ran while one was open for 0% -> 0% of each run, Pallas kernels for 0% -> 3%
where the time goes in v5:
time: 97.4 us; the launch traced here: 97 us
  Pallas kernels  40.1 us (41%)
  starting transfers between devices  23.4 us (24%)
  waiting for transfers between devices  18 us (18%)
  blocking collectives  15.5 us (16%)
    pallas_call x1, Pallas kernels, pair_sums(): pl.pallas_call(functools.partial(pair_kernel, tile, unroll), out_shape=ja...  33.2 us
    all_to_all x2, starting transfers between devices, exchange(): lax.all_to_all(blocks, AXES, 0, 0, axis_index_groups=groups, tiled=True)  23.4 us
    all_to_all x2, waiting for transfers between devices, exchange(): lax.all_to_all(blocks, AXES, 0, 0, axis_index_groups=groups, tiled=True)  18 us
    all_to_all x1, blocking collectives, exchange(): lax.all_to_all(blocks, AXES, 0, 0, axis_index_groups=groups, tiled=True)  15.5 us
    pallas_call x3, Pallas kernels, small_call(): pl.pallas_call(kernel, out_shape=tuple((jax.ShapeDtypeStruct(shape, F32)...  5.47 us
  transfers between devices with their start and end apart: 2, of which 2 were waited for; matrix products, arithmetic and copies ran while one was open for 0% of the time, Pallas kernels for 3%

profile of v5, /device:TPU:1, one launch (start us, length us, event | category | flops | bytes accessed | tf_op | source)
XLA Modules:
  0.0 97.0 jit_solution(8910051943281679695)
XLA Ops:
  0.0 1.8 %pack_plane.1 = f32[32,16,128]{2,1,0:T(8,128)} custom-call(f32[9,128]{1,0:T(8,128)} %phase.3, f32[1,128]{1,0:T(1,128)} %bitcast.5, s32[1,128]{1,0:T(1,128)} %bitcast.2), custom_call_target="tpu_custom_call" | custom-call | tf_op jit(solution)/shard_map/pack_plane/pallas_call | solution.py:263
  1.8 10.4 %all-to-all-start = ((f32[32,16,128]{2,1,0:T(8,128)}), f32[32,16,128]{2,1,0:T(8,128)S(1)}, u32[]{:S(2)}, u32[]{:S(2)}) async-start(f32[32,16,128]{2,1,0:T(8,128)} %pack_plane.1), calls=%async_computation | async-start | bytes 524288 | tf_op jit(solution)/shard_map/all_to_all | solution.py:288
  12.2 1.8 %pack_line.1 = f32[16,16,128]{2,1,0:T(8,128)} custom-call(f32[9,128]{1,0:T(8,128)} %phase.3, f32[1,128]{1,0:T(1,128)} %bitcast.6, s32[1,128]{1,0:T(1,128)} %bitcast.3), custom_call_target="tpu_custom_call" | custom-call | tf_op jit(solution)/shard_map/pack_line/pallas_call | solution.py:263
  14.0 7.2 %all-to-all-done.targets = f32[32,16,128]{2,1,0:T(8,128)S(1)} async-done(((f32[32,16,128]{2,1,0:T(8,128)}), f32[32,16,128]{2,1,0:T(8,128)S(1)}, u32[]{:S(2)}, u32[]{:S(2)}) %all-to-all-start) | async-done | bytes 262176 | tf_op jit(solution)/shard_map/all_to_all | solution.py:288
  21.2 13.0 %all-to-all-start.1 = ((f32[16,16,128]{2,1,0:T(8,128)}), f32[16,16,128]{2,1,0:T(8,128)S(1)}, u32[]{:S(2)}, u32[]{:S(2)}) async-start(f32[16,16,128]{2,1,0:T(8,128)} %pack_line.1), calls=%async_computation.1 | async-start | bytes 262144 | tf_op jit(solution)/shard_map/all_to_all | solution.py:288
  34.2 1.4 %prepare_targets.1 = (f32[34,16,128]{2,1,0:T(8,128)S(1)}, bf16[96,4096]{1,0:T(8,128)(2,1)S(1)}, bf16[96,4096]{1,0:T(8,128)(2,1)S(1)}, s32[33]{0:T(128)S(1)}) custom-call(f32[32,16,128]{2,1,0:T(8,128)S(1)} %all-to-all-done.targets), custom_call_target="tpu_custom_call" | custom-call | tf_op jit(solution)/shard_map/prepare_targets/pallas_call | solution.py:187
  35.6 10.7 %all-to-all-done.1.sources = f32[16,16,128]{2,1,0:T(8,128)S(1)} async-done(((f32[16,16,128]{2,1,0:T(8,128)}), f32[16,16,128]{2,1,0:T(8,128)S(1)}, u32[]{:S(2)}, u32[]{:S(2)}) %all-to-all-start.1) | async-done | bytes 131104 | tf_op jit(solution)/shard_map/all_to_all | solution.py:288
  46.4 33.2 %pair_sums.1 = f32[32,9,128]{2,1,0:T(8,128)S(1)} custom-call(f32[34,16,128]{2,1,0:T(8,128)S(1)} %get-tuple-element.9.due, bf16[96,4096]{1,0:T(8,128)(2,1)S(1)} %get-tuple-element.10.left_rate, bf16[96,4096]{1,0:T(8,128)(2,1)S(1)} %get-tuple-element.11.left_second, s32[33]{0:T(128)S(1)} %get-tuple-element.12.starts, f32[16,16,128]{2,1,0:T(8,128)S(1)} %all-to-all-done.1.sources), custom_call_target="tpu_custom_call" | custom-call | tf_op jit(solution)/shard_map/pair_sums/pallas_call | solution.py:207
  79.6 15.5 %all_to_all.15.sums = f32[32,9,128]{2,1,0:T(8,128)} all-to-all(f32[32,9,128]{2,1,0:T(8,128)S(1)} %pair_sums.1), channel_id=1, replica_groups={{0,1,2,3,16,17,18,19,32,33,34,35,48,49,50,51,64,65,66,67,80,81,82,83,96..., dimensions={0} | all-to-all | bytes 294912 | tf_op jit(solution)/shard_map/all_to_all | solution.py:288
  95.1 1.9 %unpack_sums.1 = f32[9,128]{1,0:T(8,128)} custom-call(f32[32,9,128]{2,1,0:T(8,128)} %all_to_all.15.sums, s32[1,128]{1,0:T(1,128)} %bitcast.4), custom_call_target="tpu_custom_call" | custom-call | tf_op jit(solution)/shard_map/unpack_sums/pallas_call | solution.py:263
Async XLA Ops:
  1.8 19.4 %all-to-all-start = ((f32[32,16,128]{2,1,0:T(8,128)}), f32[32,16,128]{2,1,0:T(8,128)S(1)}, u32[]{:S(2)}, u32[]{:S(2)}) async-start(f32[32,16,128]{2,1,0:T(8,128)} %pack_plane.1), calls=%async_computation | async-start | bytes 524288 | tf_op jit(solution)/shard_map/all_to_all | solution.py:288
  21.2 25.2 %all-to-all-start.1 = ((f32[16,16,128]{2,1,0:T(8,128)}), f32[16,16,128]{2,1,0:T(8,128)S(1)}, u32[]{:S(2)}, u32[]{:S(2)}) async-start(f32[16,16,128]{2,1,0:T(8,128)} %pack_line.1), calls=%async_computation.1 | async-start | bytes 262144 | tf_op jit(solution)/shard_map/all_to_all | solution.py:288

commit v6 on v5

--- a/solution.py
+++ b/solution.py
@@ -115,7 +115,7 @@
         feats[:, lanes] = stage[...].astype(BF16)
         return carry
 
-    lax.fori_loop(0, source_blocks // WIDE, prepare_sources, 0)
+    lax.fori_loop(0, source_blocks // WIDE, prepare_sources, 0, unroll=True)
     totals[...] = jnp.zeros_like(totals)
     turns = source_count // (tile * unroll)
 
@@ -172,7 +172,7 @@
         )
         return carry
 
-    lax.fori_loop(0, pairs_of_blocks * 2 + odd_block, finish, 0)
+    lax.fori_loop(0, target_blocks, finish, 0, unroll=True)
 
     lane = lax.broadcasted_iota(jnp.int32, (16, LANES), 1)
     for k in range(target_blocks):

time: 97.4 us -> 96.3 us (0.989)
  no operation moved by 1% of the time
where the time goes in v6:
time: 96.3 us; the launch traced here: 96.6 us
  Pallas kernels  39.7 us (41%)
  starting transfers between devices  23.4 us (24%)
  waiting for transfers between devices  18 us (19%)
  blocking collectives  15.5 us (16%)
    pallas_call x1, Pallas kernels, pair_sums(): pl.pallas_call(functools.partial(pair_kernel, tile, unroll), out_shape=ja...  32.8 us
    all_to_all x2, starting transfers between devices, exchange(): lax.all_to_all(blocks, AXES, 0, 0, axis_index_groups=groups, tiled=True)  23.4 us
    all_to_all x2, waiting for transfers between devices, exchange(): lax.all_to_all(blocks, AXES, 0, 0, axis_index_groups=groups, tiled=True)  18 us
    all_to_all x1, blocking collectives, exchange(): lax.all_to_all(blocks, AXES, 0, 0, axis_index_groups=groups, tiled=True)  15.5 us
    pallas_call x3, Pallas kernels, small_call(): pl.pallas_call(kernel, out_shape=tuple((jax.ShapeDtypeStruct(shape, F32)...  5.47 us
  transfers between devices with their start and end apart: 2, of which 2 were waited for; matrix products, arithmetic and copies ran while one was open for 0% of the time, Pallas kernels for 3%

profile of v6, /device:TPU:1, one launch (start us, length us, event | category | flops | bytes accessed | tf_op | source)
XLA Modules:
  0.0 96.6 jit_solution(3179110432071008956)
XLA Ops:
  0.0 1.8 %pack_plane.1 = f32[32,16,128]{2,1,0:T(8,128)} custom-call(f32[9,128]{1,0:T(8,128)} %phase.3, f32[1,128]{1,0:T(1,128)} %bitcast.5, s32[1,128]{1,0:T(1,128)} %bitcast.2), custom_call_target="tpu_custom_call" | custom-call | tf_op jit(solution)/shard_map/pack_plane/pallas_call | solution.py:263
  1.8 10.4 %all-to-all-start = ((f32[32,16,128]{2,1,0:T(8,128)}), f32[32,16,128]{2,1,0:T(8,128)S(1)}, u32[]{:S(2)}, u32[]{:S(2)}) async-start(f32[32,16,128]{2,1,0:T(8,128)} %pack_plane.1), calls=%async_computation | async-start | bytes 524288 | tf_op jit(solution)/shard_map/all_to_all | solution.py:288
  12.2 1.8 %pack_line.1 = f32[16,16,128]{2,1,0:T(8,128)} custom-call(f32[9,128]{1,0:T(8,128)} %phase.3, f32[1,128]{1,0:T(1,128)} %bitcast.6, s32[1,128]{1,0:T(1,128)} %bitcast.3), custom_call_target="tpu_custom_call" | custom-call | tf_op jit(solution)/shard_map/pack_line/pallas_call | solution.py:263
  14.0 7.2 %all-to-all-done.targets = f32[32,16,128]{2,1,0:T(8,128)S(1)} async-done(((f32[32,16,128]{2,1,0:T(8,128)}), f32[32,16,128]{2,1,0:T(8,128)S(1)}, u32[]{:S(2)}, u32[]{:S(2)}) %all-to-all-start) | async-done | bytes 262176 | tf_op jit(solution)/shard_map/all_to_all | solution.py:288
  21.2 13.0 %all-to-all-start.1 = ((f32[16,16,128]{2,1,0:T(8,128)}), f32[16,16,128]{2,1,0:T(8,128)S(1)}, u32[]{:S(2)}, u32[]{:S(2)}) async-start(f32[16,16,128]{2,1,0:T(8,128)} %pack_line.1), calls=%async_computation.1 | async-start | bytes 262144 | tf_op jit(solution)/shard_map/all_to_all | solution.py:288
  34.2 1.4 %prepare_targets.1 = (f32[34,16,128]{2,1,0:T(8,128)S(1)}, bf16[96,4096]{1,0:T(8,128)(2,1)S(1)}, bf16[96,4096]{1,0:T(8,128)(2,1)S(1)}, s32[33]{0:T(128)S(1)}) custom-call(f32[32,16,128]{2,1,0:T(8,128)S(1)} %all-to-all-done.targets), custom_call_target="tpu_custom_call" | custom-call | tf_op jit(solution)/shard_map/prepare_targets/pallas_call | solution.py:187
  35.6 10.7 %all-to-all-done.1.sources = f32[16,16,128]{2,1,0:T(8,128)S(1)} async-done(((f32[16,16,128]{2,1,0:T(8,128)}), f32[16,16,128]{2,1,0:T(8,128)S(1)}, u32[]{:S(2)}, u32[]{:S(2)}) %all-to-all-start.1) | async-done | bytes 131104 | tf_op jit(solution)/shard_map/all_to_all | solution.py:288
  46.4 32.8 %pair_sums.1 = f32[32,9,128]{2,1,0:T(8,128)S(1)} custom-call(f32[34,16,128]{2,1,0:T(8,128)S(1)} %get-tuple-element.9.due, bf16[96,4096]{1,0:T(8,128)(2,1)S(1)} %get-tuple-element.10.left_rate, bf16[96,4096]{1,0:T(8,128)(2,1)S(1)} %get-tuple-element.11.left_second, s32[33]{0:T(128)S(1)} %get-tuple-element.12.starts, f32[16,16,128]{2,1,0:T(8,128)S(1)} %all-to-all-done.1.sources), custom_call_target="tpu_custom_call" | custom-call | tf_op jit(solution)/shard_map/pair_sums/pallas_call | solution.py:207
  79.2 15.5 %all_to_all.15.sums = f32[32,9,128]{2,1,0:T(8,128)} all-to-all(f32[32,9,128]{2,1,0:T(8,128)S(1)} %pair_sums.1), channel_id=1, replica_groups={{0,1,2,3,16,17,18,19,32,33,34,35,48,49,50,51,64,65,66,67,80,81,82,83,96..., dimensions={0} | all-to-all | bytes 294912 | tf_op jit(solution)/shard_map/all_to_all | solution.py:288
  94.7 1.9 %unpack_sums.1 = f32[9,128]{1,0:T(8,128)} custom-call(f32[32,9,128]{2,1,0:T(8,128)} %all_to_all.15.sums, s32[1,128]{1,0:T(1,128)} %bitcast.4), custom_call_target="tpu_custom_call" | custom-call | tf_op jit(solution)/shard_map/unpack_sums/pallas_call | solution.py:263
Async XLA Ops:
  1.8 19.4 %all-to-all-start = ((f32[32,16,128]{2,1,0:T(8,128)}), f32[32,16,128]{2,1,0:T(8,128)S(1)}, u32[]{:S(2)}, u32[]{:S(2)}) async-start(f32[32,16,128]{2,1,0:T(8,128)} %pack_plane.1), calls=%async_computation | async-start | bytes 524288 | tf_op jit(solution)/shard_map/all_to_all | solution.py:288
  21.2 25.2 %all-to-all-start.1 = ((f32[16,16,128]{2,1,0:T(8,128)}), f32[16,16,128]{2,1,0:T(8,128)S(1)}, u32[]{:S(2)}, u32[]{:S(2)}) async-start(f32[16,16,128]{2,1,0:T(8,128)} %pack_line.1), calls=%async_computation.1 | async-start | bytes 262144 | tf_op jit(solution)/shard_map/all_to_all | solution.py:288
